TPU v7x, 512 devices: a whole 4x4x16 slice. The times are simulated.
512 devices in a mesh: paths: 8 (over y, core), tm: 64 (over z, x).
Axes of the slice: x: 4, y: 4, z: 16, core: 2. Of those that a mesh axis runs over, the one named last changes fastest.
Arguments:
- independent_disturbances: bfloat16 [4096, 32, 1024], P('tm', 'paths'), may hold values from -6 to 6
- starting_driver_values: float32 [32, 1024], P('paths'), may hold values from -6 to 6
- correlation_mixer: bfloat16 [1024, 1024], P('paths'), may hold values from -0.1875 to 0.1875
- log_persistence: float32 [1024], replicated, may hold values from -0.034 to 0
- regime_multiplier: float32 [4096], P('tm'), may hold values from 0.5 to 1
- payoff_per_unit_table: bfloat16 [1024, 128], replicated, may hold values from -0.1875 to 0.1875
- short_yield_coefficients: bfloat16 [1024], replicated, may hold values from -0.1875 to 0.1875
Outputs:
- values: float32 [32, 128], P('paths')
All inputs are finite; a program needn't handle non-finite values.
Results may differ from a plain program's by a relative error of at most 0.0004.
Values may be sent and summed in bfloat16 or wider, within the bound.
A program may use at most 64 MiB of HBM per device.

v0:
```python
import jax
import jax.numpy as jnp
from jax import lax
from jax.sharding import Mesh
from jax.sharding import PartitionSpec as P

TM = ("tm_0", "tm_1")


def filled_with(shard, identity):
    return jax.tree.map(
        lambda a, e: jnp.broadcast_to(jnp.asarray(e, a.dtype), a.shape), shard, identity
    )


def all_in_one(shard, axis):
    leaves = jax.tree.leaves(shard)
    sequence = sorted(range(len(leaves)), key=lambda k: -leaves[k].size)
    width = (1, *leaves[sequence[0]].shape)[-1]
    lines = [
        jnp.pad(leaves[k].reshape(-1), (0, -leaves[k].size % width)).reshape(-1, width)
        for k in sequence
    ]
    both, at, found = (lax.all_gather(jnp.concatenate(lines), axis), 0, {})
    for k, line in zip(sequence, lines):
        piece = both[:, at : at + len(line)].reshape(len(both), -1)
        found[k] = piece[:, : leaves[k].size].reshape(-1, *leaves[k].shape)
        at += len(line)
    numbers = iter(range(len(leaves)))
    return jax.tree.map(lambda _: found[next(numbers)], shard)


def carried_in(shard, axes, combine, identity):
    before = start = filled_with(shard, identity)
    running = shard
    for axis in reversed(axes):
        peers, here = (lax.axis_size(axis), lax.axis_index(axis))
        pieces = all_in_one(running, axis)
        inside, running = (start, start)
        for k in range(peers):
            passed = k < here
            running = combine(running, jax.tree.map(lambda part: part[k], pieces))
            inside = jax.tree.map(lambda new, old: jnp.where(passed, new, old), running, inside)
        before = combine(inside, before)
    return before


def copy_for_each(shard, axis):
    copies = jnp.broadcast_to(shard, (lax.axis_size(axis), *shard.shape))
    return lax.all_to_all(copies, axis, split_axis=0, concat_axis=0, tiled=True)


def combined_pairwise(pieces, combine):
    while len(jax.tree.leaves(pieces)[0]) > 1:
        pieces = jax.vmap(combine)(*(pieces[side::2] for side in (0, 1)))
    return pieces[0]


def prefix(shard, axis, combine, identity):
    peers, here = (lax.axis_size(axis), lax.axis_index(axis))
    passed = jnp.arange(peers) < here

    def kept(part, zero, own):
        part = jnp.where(
            passed.reshape(-1, *(1 for _ in own.shape)), part, jnp.asarray(zero, own.dtype)
        )
        return part

    pieces = copy_for_each(shard, axis)
    return combined_pairwise(kept(pieces, identity, shard), combine)


def of_everyone(shard, axis):
    return copy_for_each(shard, axis).sum(axis=0)


def local(
    independent_disturbances,
    starting_driver_values,
    correlation_mixer,
    log_persistence,
    regime_multiplier,
    payoff_per_unit_table,
    short_yield_coefficients,
):
    slab_days, group_paths, driver_value_history = independent_disturbances.shape
    where_now = lax.axis_index(TM)
    correlated_disturbances = jnp.einsum(
        "spf,fg->spg",
        independent_disturbances,
        lax.all_gather(correlation_mixer, "paths", axis=0, tiled=True),
        preferred_element_type=jnp.float32,
    )
    persistence_multiplier = jnp.exp(log_persistence)
    vol = jnp.sqrt(-jnp.expm1(2.0 * log_persistence))
    leading_element = jnp.where(
        where_now == 0, starting_driver_values, jnp.zeros_like(starting_driver_values)
    )

    def propagate_one_day(carry, operand_tensors):
        state, decay = carry
        random_normal_sample, regime_multiplier_today = operand_tensors
        driver_value_now = persistence_multiplier * regime_multiplier_today
        state = driver_value_now * state + vol * random_normal_sample
        decay = decay * driver_value_now
        return ((state, decay), (state, decay))

    (state, decay), (local_states, local_decays) = lax.scan(
        propagate_one_day,
        (leading_element, jnp.ones((driver_value_history,), jnp.float32)),
        (correlated_disturbances, regime_multiplier),
    )

    def chain(earlier, later):
        return (earlier[0] * later[0], later[0][None, :] * earlier[1] + later[1])

    identity = (
        jnp.ones((driver_value_history,), jnp.float32),
        jnp.zeros((group_paths, driver_value_history), jnp.float32),
    )
    carried = carried_in((decay, state), TM, chain, identity)
    driver_trajectory = local_states + local_decays[:, None, :] * carried[1][None, :, :]
    scenario = driver_trajectory.astype(jnp.bfloat16)
    horizon_days = slab_days * lax.axis_size(TM)
    cash = jnp.einsum(
        "tpf,fk->tpk", scenario, payoff_per_unit_table, preferred_element_type=jnp.float32
    )
    rate = 0.03 + 0.3 * jnp.einsum(
        "tpf,f->tp", scenario, short_yield_coefficients, preferred_element_type=jnp.float32
    )
    running = jnp.cumsum(rate, axis=0)

    def added(earlier, later):
        return earlier + later

    before = prefix(running[-1], TM, added, jnp.zeros((group_paths,), jnp.float32))
    discount = jnp.exp(-(1.0 / 256.0) * (before[None, :] + running))
    partial_sum = jnp.sum(discount[:, :, None] * cash, axis=0) / horizon_days
    return of_everyone(partial_sum, TM)


def solution(mesh):
    split = Mesh(mesh.devices.reshape(mesh.shape["paths"], 16, 4), ("paths", "tm_0", "tm_1"))
    placed = (P(TM, "paths", None), P("paths", None), P("paths", None), P(), P(TM), P(), P())
    return jax.shard_map(
        local, mesh=split, in_specs=placed, out_specs=P("paths", None), check_vma=False
    )
```

profile of v0, /device:TPU:2, one launch (start us, length us, event | category | flops | bytes accessed | tf_op | source)
XLA Modules:
  0.0 236.4 jit_solution(2021905275992335647)
XLA Ops:
  6.5 0.7 all-gather.6.cloned.1.call-update
  7.3 0.7 reshape.283
  8.0 0.7 negate_sqrt_fusion
  8.8 38.1 %all-gather.6.cloned.1.call-done = bf16[1024,1024]{1,0:T(8,128)(2,1)} async-done(((bf16[128,1024]{1,0:T(8,128)(2,1)}), bf16[1024,1024]{1,0:T(8,128)(2,1)}) %all-gather.6.cloned.1.call-update) | async-done | bytes 2097168 | tf_op jit(solution)/shard_map/all_gather | solution.py:91
  46.9 2.5 %fusion.2 = f32[64,4,1024]{2,0,1:T(8,128)S(1)} fusion(bf16[1024,1024]{1,0:T(8,128)(2,1)} %all-gather.6.cloned.1.call-done, bf16[64,4,1024]{2,1,0:T(4,128)(2,1)} %param.9), kind=kOutput, calls=%fused_computation.7 | convolution fusion | flops 536870912 | bytes 3670016 | tf_op jit(solution)/shard_map/spf,fg->spg/dot_general | solution.py:88
  49.4 85.9 %while.17 = (s32[]{:T(128)}, f32[4,1024]{1,0:T(4,128)S(1)}, f32[1024]{0:T(1024)S(1)}, f32[64,4,1024]{2,1,0:T(4,128)S(1)}, f32[64,1024]{1,0:T(8,128)S(1)}, /*inde...) while((s32[]{:T(128)}, f32[4,1024]{1,0:T(4,128)S(1)}, ...), condition=%wide.region_1.2_spmd.clone, body=%wide.region_0.1_spmd.clone.sunk | while | flops 15363 | bytes 131219 | solution.py:108
  49.4 0.6 dynamic_slice.14
  50.7 0.6 dynamic_slice.14
  52.1 0.6 dynamic_slice.14
  54.7 0.6 dynamic_slice.14
  57.4 0.6 dynamic_slice.14
  58.8 0.6 dynamic_slice.14
  60.1 0.6 dynamic_slice.14
  61.5 0.6 dynamic_slice.14
  64.1 0.6 dynamic_slice.14
  66.8 0.6 dynamic_slice.14
  68.2 0.6 dynamic_slice.14
  70.9 0.6 dynamic_slice.14
  73.5 0.6 dynamic_slice.14
  74.9 0.6 dynamic_slice.14
  76.2 0.6 dynamic_slice.14
  77.6 0.6 dynamic_slice.14
  80.3 0.6 dynamic_slice.14
  82.9 0.6 dynamic_slice.14
  84.3 0.6 dynamic_slice.14
  135.3 12.2 %all-gather.2 = f32[4,5,1024]{2,1,0:T(8,128)S(1)} all-gather(f32[1,5,1024]{2,1,0:T(8,128)S(1)} %maximum_bitcast_fusion), channel_id=2, replica_groups=mesh['paths'=8,'tm_0'=16,'tm_1'=4] {'tm_1'}, dimensions={0}, use_global_device_ids=true | all-gather | bytes 102400 | tf_op jit(solution)/shard_map/all_gather | solution.py:24
  147.6 33.2 %all-gather.3 = f32[16,5,1024]{2,1,0:T(8,128)S(1)} all-gather(f32[1,5,1024]{2,1,0:T(8,128)S(1)} %maximum_bitcast_fusion.1), channel_id=3, replica_groups=mesh['paths'=8,'tm_0'=16,'tm_1'=4] {'tm_0'}, dimensions={0}, use_global_device_ids=true | all-gather | bytes 348160 | tf_op jit(solution)/shard_map/all_gather | solution.py:24
  181.9 0.6 broadcast_in_dim.41
  182.5 11.7 %all-to-all-start = ((f32[64,1,4]{2,1,0:T(1,128)}), f32[64,1,4]{2,1,0:T(1,128)S(1)}, u32[]{:S(2)}, u32[]{:S(2)}) async-start(f32[64,1,4]{2,1,0:T(1,128)} %broadcast_in_dim.41), calls=%async_computation | async-start | bytes 65536 | tf_op jit(solution)/shard_map/all_to_all | solution.py:50
  194.3 13.8 %all-to-all-done = f32[64,1,4]{2,1,0:T(1,128)S(1)} async-done(((f32[64,1,4]{2,1,0:T(1,128)}), f32[64,1,4]{2,1,0:T(1,128)S(1)}, u32[]{:S(2)}, u32[]{:S(2)}) %all-to-all-start) | async-done | bytes 1056 | tf_op jit(solution)/shard_map/all_to_all | solution.py:50
  208.8 20.1 %all_to_all.14 = f32[64,4,128]{2,1,0:T(4,128)S(1)} all-to-all(f32[64,4,128]{2,1,0:T(4,128)S(1)} %broadcast_in_dim.43), channel_id=1, replica_groups=mesh['paths'=8,'tm_0'=16,'tm_1'=4] {'tm_0','tm_1'}, dimensions={0} | all-to-all | bytes 262144 | tf_op jit(solution)/shard_map/all_to_all | solution.py:50
  228.9 0.7 reduce_sum.19
  (346 shorter events, 74.1 us)
Async XLA Ops:
  6.5 201.9 %copy-start = (bf16[1024,128]{1,0:T(8,128)(2,1)S(1)}, bf16[1024,128]{1,0:T(8,128)(2,1)}, u32[]{:S(2)}) copy-start(bf16[1024,128]{1,0:T(8,128)(2,1)} %param.14) | copy-start | bytes 786436
  6.5 42.8 %copy-start.1 = (f32[64]{0:T(128)S(1)}, f32[64]{0:T(128)}, u32[]{:S(2)}) copy-start(f32[64]{0:T(128)} %param.13) | copy-start | bytes 772
  6.5 40.3 %all-gather.6.cloned.1.call-start = ((), (), s32[]{:S(2)}) async-start(), calls=%async_computation.2 | async-start | bytes 2359296 | tf_op jit(solution)/shard_map/all_gather | solution.py:91
  182.5 25.5 %all-to-all-start = ((f32[64,1,4]{2,1,0:T(1,128)}), f32[64,1,4]{2,1,0:T(1,128)S(1)}, u32[]{:S(2)}, u32[]{:S(2)}) async-start(f32[64,1,4]{2,1,0:T(1,128)} %broadcast_in_dim.41), calls=%async_computation | async-start | bytes 65536 | tf_op jit(solution)/shard_map/all_to_all | solution.py:50
Sparse Core Ops, SparseCore 0:
  9.5 37.2 all-gather.5
where the time goes:
time: 237 us; the launch traced here: 236 us
  blocking collectives  65.5 us (28%)
  waiting for transfers between devices  52.6 us (22%)
  local copies, waits for them, and re-layouts  47.2 us (20%)
  other arithmetic  39.9 us (17%)
  between operations  13.6 us (6%)
  starting transfers between devices  11.7 us (5%)
  matrix products  3.15 us (1%)
  loops' own time  2.69 us (1%)
    all_gather x2, blocking collectives, all_in_one(): both, at, found = (lax.all_gather(jnp.concatenate(lines), axis), 0, {})  45.4 us
    dynamic_slice x128, local copies, waits for them, and re-layouts, local(): lax.scan(propagate_one_day, (leading_element, jnp.ones((driver_value_hist...  38.5 us
    all_gather x1, waiting for transfers between devices, local(): lax.all_gather(correlation_mixer, 'paths', axis=0, tiled=True)  38.1 us
    mul x64, other arithmetic, propagate_one_day(): decay = decay * driver_value_now  36 us
    all_to_all x1, blocking collectives, copy_for_each(): return lax.all_to_all(copies, axis, split_axis=0, concat_axis=0, tiled=True)  20.1 us
    all_to_all x1, waiting for transfers between devices, copy_for_each(): return lax.all_to_all(copies, axis, split_axis=0, concat_axis=0, tiled=True)  13.8 us
    all_to_all x1, starting transfers between devices, copy_for_each(): return lax.all_to_all(copies, axis, split_axis=0, concat_axis=0, tiled=True)  11.7 us
    dynamic_update_slice x64, local copies, waits for them, and re-layouts, local(): lax.scan(propagate_one_day, (leading_element, jnp.ones((driver_value_hist...  7.04 us
  transfers between devices with their start and end apart: 2, of which 2 were waited for; matrix products, arithmetic and copies ran while one was open for 1% of the time, Pallas kernels for 0%

commit v1 on v0

--- a/solution.py
+++ b/solution.py
@@ -5,6 +5,19 @@
 from jax.sharding import PartitionSpec as P
 
 TM = ("tm_0", "tm_1")
+
+
+def ring_gather(value, axis, dim):
+    ways = lax.axis_size(axis)
+    up = [(d, (d + 1) % ways) for d in range(ways)]
+    down = [(d, (d - 1) % ways) for d in range(ways)]
+    earlier, later = ([value], [value])
+    for _ in range(ways // 2):
+        earlier.append(lax.ppermute(earlier[-1], axis, up))
+    for _ in range((ways - 1) // 2):
+        later.append(lax.ppermute(later[-1], axis, down))
+    line = jnp.concatenate([*earlier[::-1], *later[1:]], axis=dim)
+    return jnp.roll(line, (lax.axis_index(axis) - ways // 2) * value.shape[dim], axis=dim)
 
 
 def filled_with(shard, identity):
@@ -88,7 +101,7 @@
     correlated_disturbances = jnp.einsum(
         "spf,fg->spg",
         independent_disturbances,
-        lax.all_gather(correlation_mixer, "paths", axis=0, tiled=True),
+        ring_gather(correlation_mixer, "paths", 0),
         preferred_element_type=jnp.float32,
     )
     persistence_multiplier = jnp.exp(log_persistence)

time: 237 us -> 222 us (0.937)
  waiting for transfers between devices: 52.6 us -> 31.8 us
  between operations: 13.6 us -> 0.42 us
  starting transfers between devices: 11.7 us -> 18.7 us
  blocking collectives: 65.5 us -> 70.5 us
  other arithmetic: 39.9 us -> 44.8 us
  local copies, waits for them, and re-layouts: 47.2 us -> 50.4 us
    all_gather x1 -> x0, waiting for transfers between devices: 38.1 us -> none  [local(): lax.all_gather(correlation_mixer, 'paths', axis=0, tiled=True)]
    ppermute x0 -> x7, waiting for transfers between devices: none -> 18 us  [the longest x4 17.6 us: ring_gather(): earlier.append(lax.ppermute(earlier[-1], axis, up))]
    ppermute x0 -> x7, starting transfers between devices: none -> 8.94 us  [the longest x3 8.93 us: ring_gather(): later.append(lax.ppermute(later[-1], axis, down))]
    all_gather x2, blocking collectives: 45.4 us -> 50.5 us  [all_in_one(): both, at, found = (lax.all_gather(jnp.concatenate(lines), axis), 0, {})]
    mul x64, other arithmetic: 36 us -> 40.8 us  [propagate_one_day(): decay = decay * driver_value_now]
  transfers between devices with their start and end apart: 2 -> 8, of which waited for: 2 -> 7; matrix products, arithmetic and copies ran while one was open for 1% -> 1% of each run, Pallas kernels for 0% -> 0%
where the time goes in v1:
time: 222 us; the launch traced here: 221 us
  blocking collectives  70.5 us (32%)
  local copies, waits for them, and re-layouts  50.4 us (23%)
  other arithmetic  44.8 us (20%)
  waiting for transfers between devices  31.8 us (14%)
  starting transfers between devices  18.7 us (8%)
  loops' own time  2.69 us (1%)
    all_gather x2, blocking collectives, all_in_one(): both, at, found = (lax.all_gather(jnp.concatenate(lines), axis), 0, {})  50.5 us
    mul x64, other arithmetic, propagate_one_day(): decay = decay * driver_value_now  40.8 us
    dynamic_slice x128, local copies, waits for them, and re-layouts, local(): lax.scan(propagate_one_day, (leading_element, jnp.ones((driver_value_hist...  40.4 us
    all_to_all x1, blocking collectives, copy_for_each(): return lax.all_to_all(copies, axis, split_axis=0, concat_axis=0, tiled=True)  20 us
    ppermute x4, waiting for transfers between devices, ring_gather(): earlier.append(lax.ppermute(earlier[-1], axis, up))  17.6 us
    all_to_all x1, waiting for transfers between devices, copy_for_each(): return lax.all_to_all(copies, axis, split_axis=0, concat_axis=0, tiled=True)  13.8 us
    all_to_all x1, starting transfers between devices, copy_for_each(): return lax.all_to_all(copies, axis, split_axis=0, concat_axis=0, tiled=True)  9.74 us
    ppermute x3, starting transfers between devices, ring_gather(): later.append(lax.ppermute(later[-1], axis, down))  8.93 us
  transfers between devices with their start and end apart: 8, of which 7 were waited for; matrix products, arithmetic and copies ran while one was open for 1% of the time, Pallas kernels for 0%

profile of v1, /device:TPU:2, one launch (start us, length us, event | category | flops | bytes accessed | tf_op | source)
XLA Modules:
  0.0 220.7 jit_solution(4697217621457346448)
XLA Ops:
  0.0 7.2 %collective-permute-done = bf16[128,1024]{1,0:T(8,128)(2,1)S(1)} collective-permute-done((bf16[128,1024]{1,0:T(8,128)(2,1)}, bf16[128,1024]{1,0:T(8,128)(2,1)S(1)}, u32[]{:S(2)}, u32[]{:S(2)}) %collective-permute-start) | collective-permute-done | bytes 262176 | tf_op jit(solution)/shard_map/ppermute | solution.py:16
  7.2 3.0 %collective-permute-start.4 = (bf16[128,1024]{1,0:T(8,128)(2,1)}, bf16[128,1024]{1,0:T(8,128)(2,1)S(1)}, u32[]{:S(2)}, u32[]{:S(2)}) collective-permute-start(bf16[128,1024]{1,0:T(8,128)(2,1)} %param.11), channel_id=1, source_target_pairs={{0,448},{64,0},{128,64},{192,128},{256,192},{320,256},{384,320},{4... | collective-permute-start | bytes 786440 | tf_op jit(solution)/shard_map/ppermute | solution.py:18
  10.2 4.1 %collective-permute-done.1 = bf16[128,1024]{1,0:T(8,128)(2,1)S(1)} collective-permute-done((bf16[128,1024]{1,0:T(8,128)(2,1)S(1)}, bf16[128,1024]{1,0:T(8,128)(2,1)S(1)}, u32[]{:S(2)}, u32[]{:S(2)}) %collective-permute-start.1) | collective-permute-done | bytes 262176 | tf_op jit(solution)/shard_map/ppermute | solution.py:16
  14.4 3.0 %collective-permute-start.5 = (bf16[128,1024]{1,0:T(8,128)(2,1)S(1)}, bf16[128,1024]{1,0:T(8,128)(2,1)S(1)}, u32[]{:S(2)}, u32[]{:S(2)}) collective-permute-start(bf16[128,1024]{1,0:T(8,128)(2,1)S(1)} %collective-permute-done.4), channel_id=1, source_target_pairs={{0,448},{64,0},{128,64},{192,128},{256,192},{320,256},{384,320},{4... | collective-permute-start | bytes 786440 | tf_op jit(solution)/shard_map/ppermute | solution.py:18
  17.4 3.8 %collective-permute-done.2 = bf16[128,1024]{1,0:T(8,128)(2,1)S(1)} collective-permute-done((bf16[128,1024]{1,0:T(8,128)(2,1)S(1)}, bf16[128,1024]{1,0:T(8,128)(2,1)S(1)}, u32[]{:S(2)}, u32[]{:S(2)}) %collective-permute-start.2) | collective-permute-done | bytes 262176 | tf_op jit(solution)/shard_map/ppermute | solution.py:16
  21.2 0.7 negate_sqrt_fusion
  22.1 0.7 reshape.283
  22.8 3.0 %collective-permute-start.6 = (bf16[128,1024]{1,0:T(8,128)(2,1)S(1)}, bf16[128,1024]{1,0:T(8,128)(2,1)S(1)}, u32[]{:S(2)}, u32[]{:S(2)}) collective-permute-start(bf16[128,1024]{1,0:T(8,128)(2,1)S(1)} %collective-permute-done.5), channel_id=1, source_target_pairs={{0,448},{64,0},{128,64},{192,128},{256,192},{320,256},{384,320},{4... | collective-permute-start | bytes 786440 | tf_op jit(solution)/shard_map/ppermute | solution.py:18
  25.7 2.5 %collective-permute-done.3 = bf16[128,1024]{1,0:T(8,128)(2,1)S(1)} collective-permute-done((bf16[128,1024]{1,0:T(8,128)(2,1)S(1)}, bf16[128,1024]{1,0:T(8,128)(2,1)S(1)}, u32[]{:S(2)}, u32[]{:S(2)}) %collective-permute-start.3) | collective-permute-done | bytes 262176 | tf_op jit(solution)/shard_map/ppermute | solution.py:16
  28.4 1.0 constant_dynamic-update-slice_fusion.11
  29.9 0.7 fusion.5
  30.7 92.7 %while.17 = (s32[]{:T(128)}, f32[4,1024]{1,0:T(4,128)S(1)}, f32[1024]{0:T(1024)S(1)}, f32[64,4,1024]{2,1,0:T(4,128)S(1)}, f32[64,1024]{1,0:T(8,128)S(1)}, /*inde...) while((s32[]{:T(128)}, f32[4,1024]{1,0:T(4,128)S(1)}, ...), condition=%wide.region_1.2_spmd.clone, body=%wide.region_0.1_spmd.clone.sunk | while | flops 15363 | bytes 131219 | solution.py:121
  31.3 0.6 select_multiply_fusion.2
  32.8 0.6 select_multiply_fusion.2
  34.2 0.6 select_multiply_fusion.2
  35.7 0.6 select_multiply_fusion.2
  37.1 0.6 select_multiply_fusion.2
  38.6 0.6 select_multiply_fusion.2
  40.0 0.6 select_multiply_fusion.2
  41.4 0.6 select_multiply_fusion.2
  42.9 0.6 select_multiply_fusion.2
  44.3 0.6 select_multiply_fusion.2
  45.8 0.6 select_multiply_fusion.2
  47.2 0.6 select_multiply_fusion.2
  48.7 0.6 select_multiply_fusion.2
  50.1 0.6 select_multiply_fusion.2
  123.4 15.4 %all-gather.2 = f32[4,5,1024]{2,1,0:T(8,128)S(1)} all-gather(f32[1,5,1024]{2,1,0:T(8,128)S(1)} %maximum_bitcast_fusion), channel_id=2, replica_groups=mesh['paths'=8,'tm_0'=16,'tm_1'=4] {'tm_1'}, dimensions={0}, use_global_device_ids=true | all-gather | bytes 102400 | tf_op jit(solution)/shard_map/all_gather | solution.py:37
  138.9 35.1 %all-gather.3 = f32[16,5,1024]{2,1,0:T(8,128)S(1)} all-gather(f32[1,5,1024]{2,1,0:T(8,128)S(1)} %maximum_bitcast_fusion.1), channel_id=3, replica_groups=mesh['paths'=8,'tm_0'=16,'tm_1'=4] {'tm_0'}, dimensions={0}, use_global_device_ids=true | all-gather | bytes 348160 | tf_op jit(solution)/shard_map/all_gather | solution.py:37
  175.7 9.7 %all-to-all-start = ((f32[64,1,4]{2,1,0:T(1,128)}), f32[64,1,4]{2,1,0:T(1,128)S(1)}, u32[]{:S(2)}, u32[]{:S(2)}) async-start(f32[64,1,4]{2,1,0:T(1,128)} %broadcast_in_dim.41), calls=%async_computation | async-start | bytes 65536 | tf_op jit(solution)/shard_map/all_to_all | solution.py:63
  185.5 13.8 %all-to-all-done = f32[64,1,4]{2,1,0:T(1,128)S(1)} async-done(((f32[64,1,4]{2,1,0:T(1,128)}), f32[64,1,4]{2,1,0:T(1,128)S(1)}, u32[]{:S(2)}, u32[]{:S(2)}) %all-to-all-start) | async-done | bytes 1056 | tf_op jit(solution)/shard_map/all_to_all | solution.py:63
  200.0 20.0 %all_to_all.14 = f32[64,4,128]{2,1,0:T(4,128)S(1)} all-to-all(f32[64,4,128]{2,1,0:T(4,128)S(1)} %broadcast_in_dim.43), channel_id=1, replica_groups=mesh['paths'=8,'tm_0'=16,'tm_1'=4] {'tm_0','tm_1'}, dimensions={0} | all-to-all | bytes 262144 | tf_op jit(solution)/shard_map/all_to_all | solution.py:63
  220.0 0.7 reduce_sum.19
  (379 shorter events, 84.3 us)
Async XLA Ops:
  0.0 29.9 %copy-start = (bf16[64,4,1024]{2,1,0:T(4,128)(2,1)S(1)}, bf16[64,4,1024]{2,1,0:T(4,128)(2,1)}, u32[]{:S(2)}) copy-start(bf16[64,4,1024]{2,1,0:T(4,128)(2,1)} %param.9) | copy-start | bytes 1572868
  0.0 29.8 %copy-start.1 = (bf16[128,1024]{1,0:T(8,128)(2,1)S(1)}, bf16[128,1024]{1,0:T(8,128)(2,1)}, u32[]{:S(2)}) copy-start(bf16[128,1024]{1,0:T(8,128)(2,1)} %param.11) | copy-start | bytes 786436
  0.0 7.2 %collective-permute-start = (bf16[128,1024]{1,0:T(8,128)(2,1)}, bf16[128,1024]{1,0:T(8,128)(2,1)S(1)}, u32[]{:S(2)}, u32[]{:S(2)}) collective-permute-start(bf16[128,1024]{1,0:T(8,128)(2,1)} %param.11), channel_id=1, source_target_pairs={{0,64},{64,128},{128,192},{192,256},{256,320},{320,384},{384,448},... | collective-permute-start | bytes 786440 | tf_op jit(solution)/shard_map/ppermute | solution.py:16
  7.2 7.0 %collective-permute-start.1 = (bf16[128,1024]{1,0:T(8,128)(2,1)S(1)}, bf16[128,1024]{1,0:T(8,128)(2,1)S(1)}, u32[]{:S(2)}, u32[]{:S(2)}) collective-permute-start(bf16[128,1024]{1,0:T(8,128)(2,1)S(1)} %collective-permute-done), channel_id=1, source_target_pairs={{0,64},{64,128},{128,192},{192,256},{256,320},{320,384},{384,448},... | collective-permute-start | bytes 786440 | tf_op jit(solution)/shard_map/ppermute | solution.py:16
  7.2 7.2 %collective-permute-start.4 = (bf16[128,1024]{1,0:T(8,128)(2,1)}, bf16[128,1024]{1,0:T(8,128)(2,1)S(1)}, u32[]{:S(2)}, u32[]{:S(2)}) collective-permute-start(bf16[128,1024]{1,0:T(8,128)(2,1)} %param.11), channel_id=1, source_target_pairs={{0,448},{64,0},{128,64},{192,128},{256,192},{320,256},{384,320},{4... | collective-permute-start | bytes 786440 | tf_op jit(solution)/shard_map/ppermute | solution.py:18
  14.2 7.0 %collective-permute-start.2 = (bf16[128,1024]{1,0:T(8,128)(2,1)S(1)}, bf16[128,1024]{1,0:T(8,128)(2,1)S(1)}, u32[]{:S(2)}, u32[]{:S(2)}) collective-permute-start(bf16[128,1024]{1,0:T(8,128)(2,1)S(1)} %collective-permute-done.1), channel_id=1, source_target_pairs={{0,64},{64,128},{128,192},{192,256},{256,320},{320,384},{384,448},... | collective-permute-start | bytes 786440 | tf_op jit(solution)/shard_map/ppermute | solution.py:16
  14.4 8.4 %collective-permute-start.5 = (bf16[128,1024]{1,0:T(8,128)(2,1)S(1)}, bf16[128,1024]{1,0:T(8,128)(2,1)S(1)}, u32[]{:S(2)}, u32[]{:S(2)}) collective-permute-start(bf16[128,1024]{1,0:T(8,128)(2,1)S(1)} %collective-permute-done.4), channel_id=1, source_target_pairs={{0,448},{64,0},{128,64},{192,128},{256,192},{320,256},{384,320},{4... | collective-permute-start | bytes 786440 | tf_op jit(solution)/shard_map/ppermute | solution.py:18
  21.2 7.0 %collective-permute-start.3 = (bf16[128,1024]{1,0:T(8,128)(2,1)S(1)}, bf16[128,1024]{1,0:T(8,128)(2,1)S(1)}, u32[]{:S(2)}, u32[]{:S(2)}) collective-permute-start(bf16[128,1024]{1,0:T(8,128)(2,1)S(1)} %collective-permute-done.2), channel_id=1, source_target_pairs={{0,64},{64,128},{128,192},{192,256},{256,320},{320,384},{384,448},... | collective-permute-start | bytes 786440 | tf_op jit(solution)/shard_map/ppermute | solution.py:16
  22.8 6.9 %collective-permute-start.6 = (bf16[128,1024]{1,0:T(8,128)(2,1)S(1)}, bf16[128,1024]{1,0:T(8,128)(2,1)S(1)}, u32[]{:S(2)}, u32[]{:S(2)}) collective-permute-start(bf16[128,1024]{1,0:T(8,128)(2,1)S(1)} %collective-permute-done.5), channel_id=1, source_target_pairs={{0,448},{64,0},{128,64},{192,128},{256,192},{320,256},{384,320},{4... | collective-permute-start | bytes 786440 | tf_op jit(solution)/shard_map/ppermute | solution.py:18
  29.7 1.0 copy-start.2
  29.7 1.0 copy-start.4
  29.9 169.7 %copy-start.3 = (bf16[1024,128]{1,0:T(8,128)(2,1)S(1)}, bf16[1024,128]{1,0:T(8,128)(2,1)}, u32[]{:S(2)}) copy-start(bf16[1024,128]{1,0:T(8,128)(2,1)} %param.14) | copy-start | bytes 786436
  175.7 23.5 %all-to-all-start = ((f32[64,1,4]{2,1,0:T(1,128)}), f32[64,1,4]{2,1,0:T(1,128)S(1)}, u32[]{:S(2)}, u32[]{:S(2)}) async-start(f32[64,1,4]{2,1,0:T(1,128)} %broadcast_in_dim.41), calls=%async_computation | async-start | bytes 65536 | tf_op jit(solution)/shard_map/all_to_all | solution.py:63
